TPU v7x, 768 devices: a whole 4x8x12 slice. The times are simulated.
768 devices in a mesh: rep: 4 (over z_hi, core), occ: 6 (over z_lo), vir: 32 (over x, y).
Axes of the slice: x: 4, y: 8, z: 12 (z_hi: 2, z_lo: 6; z = z_hi * 6 + z_lo), core: 2. Of those that a mesh axis runs over, the one named last changes fastest.
Arguments:
- amplitudes: bfloat16 [3072, 12288], P('occ', ('rep', 'vir')), may hold values from -6 to 6
- ladder_ints: bfloat16 [12288, 12288], P('rep', 'vir'), may hold values from -0.15625 to 0.15625
- cycle_ints: bfloat16 [3072, 3072], P('occ'), may hold values from -0.3125 to 0.3125
- occ_irrep: int32 [3072], replicated, may hold values from 0 to 7
- vir_irrep: int32 [12288], replicated, may hold values from 0 to 7
Outputs:
- residual_update: bfloat16 [3072, 12288], P('occ', 'vir')
Inputs may be any that keep to these rules, and one draw needn't show every extreme that they name: `occ_irrep`: irrep labels of the point group. `vir_irrep`: irrep labels of the point group; the sectors are of unequal sizes.
All inputs are finite; a program needn't handle non-finite values.
Results may differ from a plain program's by a relative error of at most 0.004.
Values may be sent and summed in bfloat16 or wider, within the bound.
A program may use at most 32 MiB of HBM per device.

v0:
```python
import jax
import jax.numpy as jnp
from jax import lax
from jax.sharding import PartitionSpec as P


def body(amplitudes, ladder_ints, cycle_ints, occ_irrep, vir_irrep):
    n_vir = lax.axis_size("vir")
    rep_pos = lax.axis_index("rep")
    vir_pos = lax.axis_index("vir")
    occ_pos = lax.axis_index("occ")
    pair_rows, own_cols = amplitudes.shape
    group_rows, vir_cols = ladder_ints.shape
    zero = jnp.zeros((), jnp.bfloat16)
    occ_own = lax.dynamic_slice_in_dim(occ_irrep, occ_pos * pair_rows, pair_rows)
    own_labels = lax.dynamic_slice_in_dim(
        vir_irrep, (rep_pos * n_vir + vir_pos) * own_cols, own_cols
    )
    sector_amps = jnp.where(occ_own[:, None] == own_labels[None, :], amplitudes, zero)
    group_labels = lax.dynamic_slice_in_dim(vir_irrep, rep_pos * group_rows, group_rows)
    column_labels = lax.dynamic_slice_in_dim(vir_irrep, vir_pos * vir_cols, vir_cols)
    sector_ladder = jnp.where(group_labels[:, None] == column_labels[None, :], ladder_ints, zero)
    sector_cycle = jnp.where(occ_own[:, None] == occ_irrep[None, :], cycle_ints, zero)
    partial_ladder = jnp.dot(
        lax.all_gather(sector_amps, "vir", axis=1, tiled=True),
        sector_ladder,
        preferred_element_type=jnp.float32,
    )
    ladder = lax.psum(partial_ladder, "rep")
    ladder_b = ladder.astype(jnp.bfloat16)
    cycle = jnp.dot(
        sector_cycle,
        lax.all_gather(ladder_b, "occ", axis=0, tiled=True),
        preferred_element_type=jnp.float32,
    )
    return (ladder + cycle).astype(jnp.bfloat16)


def solution(mesh):
    in_specs = (P("occ", ("rep", "vir")), P("rep", "vir"), P("occ", None), P(), P())
    out_specs = P("occ", "vir")
    return jax.shard_map(body, mesh=mesh, in_specs=in_specs, out_specs=out_specs, check_vma=False)
```

profile of v0, /device:TPU:1, one launch (start us, length us, event | category | flops | bytes accessed | tf_op | source)
XLA Modules:
  0.0 282.6 jit_solution(304799566839032928)
XLA Ops:
  6.5 0.0 all-gather.3.cloned.1.call-start
  6.5 0.8 dynamic_slice.13
  7.3 0.8 dynamic_slice.12
  8.1 1.6 compare_select_fusion.8
  9.7 0.0 all-gather.3.cloned.1.call-update
  9.7 0.0 all-reduce.2.cloned.1.call-start
  9.8 0.8 dynamic_slice.15
  10.5 0.7 dynamic_slice.14
  11.3 0.0 copy-start
  11.3 0.0 copy-start.1
  11.3 94.5 %all-gather.3.cloned.1.call-done = bf16[512,3072]{0,1:T(8,128)(2,1)} async-done(((bf16[512,96]{0,1:T(8,128)(2,1)}), bf16[512,3072]{0,1:T(8,128)(2,1)}) %all-gather.3.cloned.1.call-update) | async-done | bytes 3145744 | tf_op jit(solution)/shard_map/all_gather | solution.py:25
  105.8 5.4 %fusion.3 = f32[512,384]{1,0:T(8,128)} fusion(bf16[512,3072]{0,1:T(8,128)(2,1)} %all-gather.3.cloned.1.call-done, bf16[3072,384]{1,0:T(8,128)(2,1)} %param.6, s32[384]{0:T(512)S(1)} %dynamic_slice.15, s32[3072]{0:T(1024)S(1)} %dynamic_slice.14), kind=kOutput, calls=%fused_computation.5 | convolution fusion | flops 1210318848 | bytes 6305280 | tf_op jit(solution)/shard_map/dot_general | solution.py:24
  111.2 0.0 all-reduce.2.cloned.1.call-update
  111.2 0.0 all-gather.5.cloned.1.call-start
  111.2 90.7 %all-reduce.2.cloned.1.call-done = f32[512,384]{1,0:T(8,128)} async-done(((f32[512,384]{1,0:T(8,128)}), f32[512,384]{1,0:T(8,128)}) %all-reduce.2.cloned.1.call-update) | async-done | bytes 786448 | tf_op jit(solution)/shard_map/psum | solution.py:29
  201.9 1.9 convert_element_type.6
  203.8 0.0 all-gather.5.cloned.1.call-update
  203.8 67.8 %all-gather.5.cloned.1.call-done = bf16[3072,384]{1,0:T(8,128)(2,1)} async-done(((bf16[512,384]{1,0:T(8,128)(2,1)}), bf16[3072,384]{1,0:T(8,128)(2,1)}) %all-gather.5.cloned.1.call-update) | async-done | bytes 2359312 | tf_op jit(solution)/shard_map/all_gather | solution.py:33
  271.6 0.0 copy-done
  271.6 0.0 copy-done.1
  271.6 4.5 %fusion.8 = bf16[512,384]{1,0:T(8,128)(2,1)} fusion(f32[512,384]{1,0:T(8,128)} %all-reduce.2.cloned.1.call-done, bf16[3072,384]{1,0:T(8,128)(2,1)} %all-gather.5.cloned.1.call-done, bf16[512,3072]{1,0:T(8,128)(2,1)S(1)} %copy-done.1, s32[3072]{0:T(1024)S(1)} %copy-done, s32[512]{0:T(512)S(1)} %dynamic_slice.12), kind=kOutput, calls=%fused_computation.10 | convolution fusion | flops 1211498496 | bytes 6699008 | tf_op jit(solution)/shard_map/dot_general | solution.py:31
Async XLA Ops:
  6.5 99.2 %all-gather.3.cloned.1.call-start = ((), (), s32[]{:S(2)}) async-start(), calls=%async_computation | async-start | bytes 3244032 | tf_op jit(solution)/shard_map/all_gather | solution.py:25
  9.7 192.2 %all-reduce.2.cloned.1.call-start = ((), (), s32[]{:S(2)}) async-start(), calls=%async_computation.1 | async-start | bytes 1572864 | tf_op jit(solution)/shard_map/psum | solution.py:29
  11.3 260.4 %copy-start = (s32[3072]{0:T(1024)S(1)}, s32[3072]{0:T(1024)}, u32[]{:S(2)}) copy-start(s32[3072]{0:T(1024)} %param.8) | copy-start | bytes 36868
  11.3 260.4 %copy-start.1 = (bf16[512,3072]{1,0:T(8,128)(2,1)S(1)}, bf16[512,3072]{1,0:T(8,128)(2,1)}, u32[]{:S(2)}) copy-start(bf16[512,3072]{1,0:T(8,128)(2,1)} %param.7) | copy-start | bytes 9437188
  111.2 160.4 %all-gather.5.cloned.1.call-start = ((), (), s32[]{:S(2)}) async-start(), calls=%async_computation.2 | async-start | bytes 2752512 | tf_op jit(solution)/shard_map/all_gather | solution.py:33
Sparse Core Ops, SparseCore 0:
  11.1 94.6 all-gather.2
  111.3 90.5 all-reduce.1
  204.3 67.2 all-gather.4
where the time goes:
time: 283 us
  waiting for transfers between devices  253 us (89%)
  between operations  13.1 us (5%)
  matrix products  9.88 us (3%)
  other arithmetic  3.55 us (1%)
  local copies, waits for them, and re-layouts  3.02 us (1%)
    all_gather x1, waiting for transfers between devices, body(): lax.all_gather(sector_amps, 'vir', axis=1, tiled=True)  94.5 us
    psum x1, waiting for transfers between devices, body(): ladder = lax.psum(partial_ladder, 'rep')  90.7 us
    all_gather x1, waiting for transfers between devices, body(): lax.all_gather(ladder_b, 'occ', axis=0, tiled=True)  67.8 us
  transfers between devices with their start and end apart: 3, of which 3 were waited for; matrix products, arithmetic and copies ran while one was open for 1% of the time, Pallas kernels for 0%

commit v1 on v0

v1 whole, which is shorter than its diff:
```python
import functools

import jax
import jax.numpy as jnp
from jax import lax
from jax.experimental import pallas as pl
from jax.experimental.pallas import tpu as pltpu
from jax.sharding import PartitionSpec as P

MESH = pl.DeviceIdType.MESH
BF, F32 = jnp.bfloat16, jnp.float32
NX, NY, NZ = 4, 8, 12
GROUPS, ROWS, CAP, LANES = 6, 512, 96, 128
OWN, COLS, DEPTH = 96, 384, 3072
HALF = CAP // 2
MAIN, SPARE = 80, LANES - CAP
Y_ORDER = (0, 1, 2, 3, 7, 6, 5, 4)
LAST_Y = Y_ORDER[-1]
Z_STEPS = (1, 2, 3, 9, 10, 11)
TOP = 32000.0


def onehot(labels):
    width = labels.shape[1]
    rows = lax.broadcasted_iota(jnp.int32, (16, width), 0)
    return jnp.where(jnp.broadcast_to(labels, (16, width)) == rows, 1.0, 0.0).astype(BF)


def meet(a, b):
    return lax.dot_general(a, b, (((0,), (0,)), ((), ())), preferred_element_type=F32)


def kernel(
    amps_in, lad_ref, cyc_ref, occ_in, vir_in, out_ref, flag_ref,
    amps_ref, occ_ref, vir_ref, lad, cyc, cbuf, racc, rin, pbuf, psc, qbuf, sbuf, ucat, lcat, omask,
    load_sem, y_send, x_send, c_recv, r_send, r_recv, q_send, s_send, q_recv, s_recv,
    g_send, gs_send, g_recv, gs_recv, f_send, fs_send, ready_x, ready_y, ready_z,
):
    rep, occ, vir = lax.axis_index("rep"), lax.axis_index("occ"), lax.axis_index("vir")
    x, y, z, core = vir // NY, vir % NY, (rep // 2) * GROUPS + occ, rep % 2

    def at(x1, y1, z1, core1):
        return {"rep": (z1 // GROUPS) * 2 + core1, "occ": z1 % GROUPS, "vir": x1 * NY + y1}

    def turn_x(x1):
        return jnp.where(x1 < 2, x1, 5 - x1)

    def turn_y(y1):
        return jnp.where(y1 < 4, y1, 11 - y1)

    def copy(src, dst, send, recv, where):
        return pltpu.make_async_remote_copy(
            src_ref=src, dst_ref=dst, send_sem=send, recv_sem=recv, device_id=where, device_id_type=MESH
        )

    loads = [
        pltpu.make_async_copy(a, b, load_sem.at[i])
        for i, (a, b) in enumerate(((occ_in, occ_ref), (vir_in, vir_ref), (amps_in, amps_ref)), 2)
    ]
    for load in loads:
        load.start()
    load_lad = pltpu.make_async_copy(lad_ref, lad, load_sem.at[0])
    load_cyc = pltpu.make_async_copy(cyc_ref, cyc, load_sem.at[1])
    load_lad.start()
    load_cyc.start()

    contacts = [((x, y1, z, core), ready_y.at[y], turn_y(y1) > turn_y(y), y1 != y) for y1 in range(NY)]
    contacts += [((x1, y, z, core), ready_x.at[x], turn_x(x1) > turn_x(x), x1 != x) for x1 in range(NX)]
    contacts += [
        ((x, y, (z + d) % NZ, core), ready_z.at[NZ - d], (z + d) % NZ > z, core < 2) for d in Z_STEPS
    ]
    barrier = pltpu.get_barrier_semaphore()
    sibling = at(x, y, z, 1 - core)
    pl.semaphore_signal(barrier, inc=1, device_id=sibling, device_id_type=MESH)
    for where, _, later, other in contacts:
        @pl.when(later & other)
        def _(where=where):
            pl.semaphore_signal(barrier, inc=1, device_id=at(*where), device_id_type=MESH)

    lower = sum(((z + d) % NZ < z).astype(jnp.int32) for d in Z_STEPS)
    pl.semaphore_wait(barrier, turn_x(x) + turn_y(y) + lower + 1)
    for where, ready, later, other in contacts:
        @pl.when(jnp.logical_not(later) & other)
        def _(where=where, ready=ready):
            pl.semaphore_signal(ready, inc=1, device_id=at(*where), device_id_type=MESH)

    for load in loads:
        load.wait()

    upper = lax.broadcasted_iota(jnp.int32, (ROWS, ROWS), 0) < lax.broadcasted_iota(jnp.int32, (ROWS, ROWS), 1)
    upper = jnp.where(upper, 1.0, 0.0).astype(BF)
    slot_ids = lax.broadcasted_iota(jnp.int32, (LANES, ROWS), 0).astype(F32)

    def slot_matrix(hot):
        before = jnp.dot(hot, upper, preferred_element_type=F32)
        rank = jnp.sum(before * hot.astype(F32), axis=0, keepdims=True)
        return jnp.where(jnp.broadcast_to(rank, (LANES, ROWS)) == slot_ids, 1.0, 0.0)

    occ_hot = onehot(occ_ref[:, pl.ds(pl.multiple_of(occ * ROWS, ROWS), ROWS)])
    own_slots = slot_matrix(occ_hot)
    first = (rep * 32 + vir) * OWN
    base = pl.multiple_of(jnp.minimum(first // 128, 94) * 128, 128)
    window = jnp.broadcast_to(vir_ref[:, pl.ds(base, 256)], (8, 256))
    window = pltpu.roll(window, (256 - (first - base)) % 256, 1)
    own_hot = onehot(window[0:1, :128])
    mask = meet(own_hot, occ_hot)[:OWN, :]
    sector = jnp.where(mask > 0.5, amps_ref[...].astype(F32), 0.0).astype(BF)

    def place(columns, slots):
        return lax.dot_general(
            columns, slots.astype(BF), (((1,), (1,)), ((), ())), preferred_element_type=F32
        )

    no_slots = jnp.zeros((SPARE, ROWS), F32)
    chunk = place(sector[:MAIN], jnp.concatenate([own_slots[:CAP], no_slots], axis=0))
    aside = [
        place(sector[MAIN:], jnp.concatenate([no_slots] * 3 + [own_slots[j * SPARE:(j + 1) * SPARE]], axis=0))
        for j in range(3)
    ]
    aside.append(jnp.zeros((MAIN - 3 * (OWN - MAIN), LANES), F32))
    cbuf[vir] = (chunk + jnp.concatenate(aside, axis=0)).astype(BF)

    def y_copy(y1):
        return copy(cbuf.at[vir], cbuf.at[vir], y_send.at[y1], c_recv.at[vir], at(x, y1, z, core))

    def x_copy(y1, d):
        v = x * NY + y1
        return copy(cbuf.at[v], cbuf.at[v], x_send.at[y1, d], c_recv.at[v], at((x + d) % NX, y, z, core))

    def c_wait(v):
        copy(cbuf.at[v], cbuf.at[v], y_send.at[0], c_recv.at[v], at(x, (y + 1) % NY, z, core)).wait_recv()

    def relay(y1):
        for d in (2, 1, 3):
            x_copy(y1, d).start()

    for y1 in Y_ORDER:
        @pl.when(turn_y(y1) < turn_y(y))
        def _(y1=y1):
            y_copy(y1).start()
    for x1 in range(NX):
        @pl.when(turn_x(x1) > turn_x(x))
        def _(x1=x1):
            pl.semaphore_wait(ready_x.at[x1], 1)
    relay(y)

    col_hot = onehot(vir_ref[:, pl.ds(pl.multiple_of(vir * COLS, 128), COLS)])

    def mask_ladder(i):
        blocks = slice(4 * i, 4 * i + 4)
        row_hot = onehot(vir_ref[:, pl.ds(pl.multiple_of(rep * DEPTH + i * COLS, 128), COLS)])
        keep = meet(row_hot, col_hot)
        rows = lad[blocks].reshape(COLS, COLS).astype(F32)
        lad[blocks] = jnp.where(keep > 0.5, rows, 0.0).astype(BF).reshape(4, OWN, COLS)

    def pack_cycle(g):
        hot = onehot(occ_ref[:, g * ROWS:(g + 1) * ROWS])
        most = jnp.max(jnp.sum(hot.astype(F32), axis=1, keepdims=True))
        group_slots = slot_matrix(hot).astype(BF)
        keep = meet(occ_hot, hot)
        part = jnp.where(keep > 0.5, cyc[:, g * ROWS:(g + 1) * ROWS].astype(F32), 0.0).astype(BF)
        moved = lax.dot_general(part, group_slots, (((1,), (1,)), ((), ())), preferred_element_type=F32)
        ucat[:, g * LANES:(g + 1) * LANES] = moved.astype(BF)
        return most

    def prepare():
        load_lad.wait()
        for i in range(8):
            mask_ladder(i)
        load_cyc.wait()
        worst = jnp.zeros((), F32)
        for g in range(GROUPS):
            worst = jnp.maximum(worst, pack_cycle(g))
        flag_ref[0] = jnp.where(worst > CAP, 1, 0)
        plain = own_slots.T.astype(BF)
        ucat[:, 6 * LANES:7 * LANES] = plain
        ucat[:, 7 * LANES:8 * LANES] = plain
        omask[...] = meet(occ_hot, col_hot)
        lcat[...] = jnp.zeros_like(lcat)

    early = turn_y(y) < 3
    pl.when(early)(prepare)
    for y1 in Y_ORDER:
        @pl.when(turn_y(y1) > turn_y(y))
        def _(y1=y1):
            pl.semaphore_wait(ready_y.at[y1], 1)
            y_copy(y1).start()
    for d in (1, 7, 2, 6, 3, 5, 4):
        source = lax.rem(y + d, NY)

        @pl.when(source != LAST_Y)
        def _(source=source):
            c_wait(x * NY + source)
            relay(source)

    @pl.when(y != LAST_Y)
    def _():
        c_wait(x * NY + LAST_Y)
        relay(LAST_Y)
    pl.when(jnp.logical_not(early))(prepare)

    def product(start):
        block, rows = cbuf[start:start + NY], lad[start:start + NY]

        def dot(a, b):
            a, b = a.reshape(-1, LANES), b.reshape(-1, COLS)
            return lax.dot_general(a, b, (((0,), (0,)), ((), ())), preferred_element_type=F32)

        main = dot(block[:, :MAIN], rows[:, :MAIN])[:CAP]
        step = OWN - MAIN
        aside = [dot(block[:, j * step:(j + 1) * step], rows[:, MAIN:])[CAP:] for j in range(3)]
        return main + jnp.concatenate(aside, axis=0)

    for x1 in range(NX):
        @pl.when(x1 != x)
        def _(x1=x1):
            for y1 in range(NY):
                c_wait(x1 * NY + y1)
    racc[...] = product(0)
    for x1 in range(1, NX):
        racc[...] += product(x1 * NY)

    mine = pl.ds(pl.multiple_of(core * HALF, HALF), HALF)
    theirs = pl.ds(pl.multiple_of((1 - core) * HALF, HALF), HALF)
    half_copy = copy(racc.at[theirs], rin, r_send, r_recv, sibling)
    half_copy.start()
    half_copy.wait_recv()
    total = racc[mine, :] + rin[...]

    def pack(values, into, scale):
        largest = jnp.max(jnp.max(jnp.abs(values), axis=1, keepdims=True), axis=0, keepdims=True)
        largest = jnp.maximum(largest, 1e-30)
        into[...] = jnp.round(values * (TOP / largest)).astype(jnp.int32).astype(jnp.int16)
        scale[...] = jnp.broadcast_to(largest * (1.0 / TOP), (8, 128))

    def unpack(packed, scale):
        return packed[...].astype(jnp.int32).astype(F32) * scale[0:1, 0:1]

    def send(q, s, to_q, to_s, sems, where):
        return copy(q, to_q, sems[0], sems[1], where), copy(s, to_s, sems[2], sems[3], where)

    def part_copy(i):
        d = (3, 9)[i]
        sems = q_send.at[i], q_recv.at[i], s_send.at[i], s_recv.at[i]
        return send(pbuf.at[2], psc.at[2], pbuf.at[i], psc.at[i], sems, at(x, y, (z + d) % NZ, core))

    group = lax.rem(z + 3, GROUPS)

    def group_copy(d):
        sems = g_send.at[d % NZ], g_recv.at[group, core], gs_send.at[d % NZ], gs_recv.at[group, core]
        to = qbuf.at[group, mine], sbuf.at[group, core]
        return send(*to, *to, sems, at(x, y, (z + d + NZ) % NZ, core))

    def side_copy(g):
        sems = f_send.at[g], g_recv.at[g, core], fs_send.at[g], gs_recv.at[g, core]
        to = qbuf.at[g, mine], sbuf.at[g, core]
        return send(*to, *to, sems, sibling)

    def group_wait(g, half):
        rows = pl.ds(pl.multiple_of(half * HALF, HALF), HALF)
        to = qbuf.at[g, rows], sbuf.at[g, half]
        sems = f_send.at[0], g_recv.at[g, half], fs_send.at[0], gs_recv.at[g, half]
        for c in send(*to, *to, sems, sibling):
            c.wait_recv()

    pack(total, pbuf.at[2], psc.at[2])
    for d in Z_STEPS:
        @pl.when((z + d) % NZ > z)
        def _(d=d):
            pl.semaphore_wait(ready_z.at[d], 1)
    for i in range(2):
        for c in part_copy(i):
            c.start()
    for i in range(2):
        for c in part_copy(i):
            c.wait_recv()
    both = unpack(pbuf.at[0], psc.at[0]) + unpack(pbuf.at[1], psc.at[1])
    pack(both, qbuf.at[group, mine], sbuf.at[group, core])
    far = jnp.where(core == 0, 3, 9)
    far_copy = [
        copy(a, a, sems[0], sems[1], at(x, y, lax.rem(z + far, NZ), core))
        for a, sems in (
            (qbuf.at[group, mine], (g_send.at[3], g_recv.at[group, core])),
            (sbuf.at[group, core], (gs_send.at[3], gs_recv.at[group, core])),
        )
    ]
    for c in far_copy:
        c.start()
    for d in (2, -2, 1, -1):
        for c in group_copy(d):
            c.start()
    for c in side_copy(group):
        c.start()
    for d in (1, -1, 2, -2, 3):
        g = lax.rem(z - d + 3 + NZ, GROUPS)
        group_wait(g, core)
        for c in side_copy(g):
            c.start()

    def whole(g):
        scale = jnp.concatenate(
            [jnp.broadcast_to(sbuf[g, h][0:1, 0:1], (HALF, COLS)) for h in range(2)], axis=0
        )
        return qbuf[g].astype(jnp.int32).astype(F32) * scale

    for g in range(GROUPS):
        group_wait(g, 1 - core)
        lcat[g * LANES:g * LANES + CAP, :] = whole(g).astype(BF)
    own = whole(occ)
    high = own.astype(BF)
    lcat[6 * LANES:6 * LANES + CAP, :] = high
    lcat[7 * LANES:7 * LANES + CAP, :] = (own - high.astype(F32)).astype(BF)
    result = jnp.dot(ucat[...], lcat[...], preferred_element_type=F32)
    out_ref[...] = jnp.where(omask[...] > 0.5, result, 0.0).astype(BF)

    for y1 in range(NY):
        @pl.when(y1 != y)
        def _(y1=y1):
            y_copy(y1).wait_send()
        for d in range(1, NX):
            x_copy(y1, d).wait_send()
    half_copy.wait_send()
    for i in range(2):
        for c in part_copy(i):
            c.wait_send()
    for c in far_copy:
        c.wait_send()
    for d in (2, -2, 1, -1):
        for c in group_copy(d):
            c.wait_send()
    for g in range(GROUPS):
        for c in side_copy(g):
            c.wait_send()


def compact(amplitudes, ladder_ints, cycle_ints, occ_irrep, vir_irrep):
    vmem, dma = pltpu.VMEM, pltpu.SemaphoreType.DMA
    return pl.pallas_call(
        kernel,
        out_shape=(jax.ShapeDtypeStruct((ROWS, COLS), BF), jax.ShapeDtypeStruct((1,), jnp.int32)),
        in_specs=[pl.BlockSpec(memory_space=pl.ANY)] * 5,
        out_specs=(pl.BlockSpec(memory_space=vmem), pl.BlockSpec(memory_space=pltpu.SMEM)),
        scratch_shapes=[
            vmem((OWN, ROWS), BF),
            vmem((1, GROUPS * ROWS), jnp.int32),
            vmem((1, NX * NY * COLS), jnp.int32),
            vmem((NX * NY, OWN, COLS), BF),
            vmem((ROWS, GROUPS * ROWS), BF),
            vmem((NX * NY, MAIN, LANES), BF),
            vmem((CAP, COLS), F32),
            vmem((HALF, COLS), F32),
            vmem((3, HALF, COLS), jnp.int16),
            vmem((3, 8, 128), F32),
            vmem((GROUPS, CAP, COLS), jnp.int16),
            vmem((GROUPS, 2, 8, 128), F32),
            vmem((ROWS, 8 * LANES), BF),
            vmem((8 * LANES, COLS), BF),
            vmem((ROWS, COLS), F32),
            dma((5,)),
            dma((NY,)),
            dma((NY, NX)),
            dma((NX * NY,)),
            dma,
            dma,
            dma((2,)),
            dma((2,)),
            dma((2,)),
            dma((2,)),
            dma((NZ,)),
            dma((NZ,)),
            dma((GROUPS, 2)),
            dma((GROUPS, 2)),
            dma((GROUPS,)),
            dma((GROUPS,)),
            pltpu.SemaphoreType.REGULAR((NX,)),
            pltpu.SemaphoreType.REGULAR((NY,)),
            pltpu.SemaphoreType.REGULAR((NZ,)),
        ],
        compiler_params=pltpu.CompilerParams(
            collective_id=0, has_side_effects=True, vmem_limit_bytes=48 * 1024 * 1024
        ),
        cost_estimate=pl.CostEstimate(flops=2_000_000_000, bytes_accessed=6_500_000, transcendentals=0),
    )(amplitudes.T, ladder_ints.reshape(NX * NY, OWN, COLS), cycle_ints, occ_irrep.reshape(1, -1), vir_irrep.reshape(1, -1))


def ring(axis, block, n):
    me = lax.axis_index(axis)
    perm = [(i, (i + 1) % n) for i in range(n)]
    held = jnp.zeros((n,) + block.shape, block.dtype)

    def step(s, carry):
        held, block = carry
        held = lax.dynamic_update_index_in_dim(held, block, (me - s + n) % n, 0)
        return held, lax.ppermute(block, axis, perm)

    held, _ = lax.fori_loop(0, n, step, (held, block))
    return held


def dense(amplitudes, ladder_ints, cycle_ints, occ_irrep, vir_irrep):
    rep_pos, vir_pos, occ_pos = lax.axis_index("rep"), lax.axis_index("vir"), lax.axis_index("occ")
    zero = jnp.zeros((), BF)
    occ_own = lax.dynamic_slice_in_dim(occ_irrep, occ_pos * ROWS, ROWS)
    own_labels = lax.dynamic_slice_in_dim(vir_irrep, (rep_pos * 32 + vir_pos) * OWN, OWN)
    sector_amps = jnp.where(occ_own[:, None] == own_labels[None, :], amplitudes, zero)
    group_labels = lax.dynamic_slice_in_dim(vir_irrep, rep_pos * DEPTH, DEPTH)
    column_labels = lax.dynamic_slice_in_dim(vir_irrep, vir_pos * COLS, COLS)
    sector_ladder = jnp.where(group_labels[:, None] == column_labels[None, :], ladder_ints, zero)
    sector_cycle = jnp.where(occ_own[:, None] == occ_irrep[None, :], cycle_ints, zero)
    gathered = ring("vir", sector_amps, NX * NY).transpose(1, 0, 2).reshape(ROWS, DEPTH)
    partial_ladder = jnp.dot(gathered, sector_ladder, preferred_element_type=F32)
    parts = ring("rep", partial_ladder, 4)
    ladder = (parts[0] + parts[1]) + (parts[2] + parts[3])
    ladder_all = ring("occ", ladder.astype(BF), GROUPS).reshape(GROUPS * ROWS, COLS)
    cycle = jnp.dot(sector_cycle, ladder_all, preferred_element_type=F32)
    return (ladder + cycle).astype(BF)


def body(*args):
    update, crowded = compact(*args)
    return lax.cond(crowded[0] > 0, lambda: dense(*args), lambda: update)


def solution(mesh):
    in_specs = (P("occ", ("rep", "vir")), P("rep", "vir"), P("occ", None), P(), P())
    return jax.shard_map(body, mesh=mesh, in_specs=in_specs, out_specs=P("occ", "vir"), check_vma=False)
```

time: 283 us -> 49.1 us (0.17)
  waiting for transfers between devices: 253 us -> 0 us
  Pallas kernels: 0 us -> 47.3 us
  between operations: 13.1 us -> 0.67 us
  matrix products: 9.88 us -> 0 us
  other arithmetic: 3.55 us -> 0 us
    all_gather x2 -> x0, waiting for transfers between devices: 162 us -> none  [the longest x1 94.5 us: body(): lax.all_gather(sector_amps, 'vir', axis=1, tiled=True)]
    psum x1 -> x0, waiting for transfers between devices: 90.7 us -> none  [body(): ladder = lax.psum(partial_ladder, 'rep')]
    pallas_call x0 -> x1, Pallas kernels: none -> 47.3 us  [compact(): pl.pallas_call(kernel, out_shape=(jax.ShapeDtypeStruct((ROWS, COLS), BF),...]
    dot_general x2 -> x0, matrix products: 9.88 us -> none  [the longest x1 5.39 us: body(): jnp.dot(lax.all_gather(sector_amps, 'vir', axis=1, tiled=True), sector_la...]
    dynamic_slice x4 -> x0, local copies, waits for them, and re-layouts: 3.01 us -> none  [the longest x1 0.78 us: body(): lax.dynamic_slice_in_dim(vir_irrep, vir_pos * vir_cols, vir_cols)]
  transfers between devices with their start and end apart: 3 -> 0, of which waited for: 3 -> 0; matrix products, arithmetic and copies ran while one was open for 1% -> 0% of each run, Pallas kernels for 0% -> 0%
where the time goes in v1:
time: 49.1 us; the launch traced here: 49 us
  Pallas kernels  47.3 us (96%)
  local copies, waits for them, and re-layouts  0.76 us (2%)
  between operations  0.67 us (1%)
    pallas_call x1, Pallas kernels, compact(): pl.pallas_call(kernel, out_shape=(jax.ShapeDtypeStruct((ROWS, COLS), BF),...  47.3 us

profile of v1, /device:TPU:1, one launch (start us, length us, event | category | flops | bytes accessed | tf_op | source)
XLA Modules:
  0.0 49.0 jit_solution(5889190112452558618)
XLA Ops:
  0.0 0.0 copy-start.1
  0.0 0.0 copy-start.2
  0.0 47.3 %shard_map.57 = (bf16[512,384]{1,0:T(8,128)(2,1)S(1)}, s32[1]{0:T(128)}) custom-call(bf16[96,512]{1,0:T(8,128)(2,1)} %bitcast.28, bf16[32,96,384]{2,1,0:T(8,128)(2,1)} %bitcast.31, bf16[512,3072]{1,0:T(8,128)(2,1)} %cyc_ref.1, s32[1,3072]{1,0:T(1,128)} %bitcast.30, s32[1,12288]{1,0:T(1,128)} %bitcast.29), custom_call_target="tpu_custom_call" | custom-call | flops 2000000000 | bytes 6500000 | tf_op jit(solution)/shard_map/pallas_call | solution.py:338
  48.0 0.0 copy-done.1
  48.0 0.0 copy-done.2
  48.0 0.2 conditional.1
  48.2 0.7 %copy.48 = bf16[512,384]{1,0:T(8,128)(2,1)} copy(bf16[512,384]{1,0:T(8,128)(2,1)S(1)} %get-tuple-element.361) | data formatting | bytes 786432
Async XLA Ops:
  0.0 48.0 %copy-start.1 = (bf16[512,96]{0,1:T(8,128)(2,1)S(1)}, bf16[512,96]{0,1:T(8,128)(2,1)}, u32[]{:S(2)}) copy-start(bf16[512,96]{0,1:T(8,128)(2,1)} %param.13) | copy-start | bytes 294916
  0.0 48.0 %copy-start.2 = (s32[3072]{0:T(1024)S(1)}, s32[3072]{0:T(1024)}, u32[]{:S(2)}) copy-start(s32[3072]{0:T(1024)} %param.16) | copy-start | bytes 36868

commit v2 on v1

--- a/solution.py
+++ b/solution.py
@@ -34,7 +34,7 @@
     amps_in, lad_ref, cyc_ref, occ_in, vir_in, out_ref, flag_ref,
     amps_ref, occ_ref, vir_ref, lad, cyc, cbuf, racc, rin, pbuf, psc, qbuf, sbuf, ucat, lcat, omask,
     load_sem, y_send, x_send, c_recv, r_send, r_recv, q_send, s_send, q_recv, s_recv,
-    g_send, gs_send, g_recv, gs_recv, f_send, fs_send, ready_x, ready_y, ready_z,
+    g_send, gs_send, g_recv, gs_recv, f_send, fs_send, ready_x, ready_y, ready_z, ready_c,
 ):
     rep, occ, vir = lax.axis_index("rep"), lax.axis_index("occ"), lax.axis_index("vir")
     x, y, z, core = vir // NY, vir % NY, (rep // 2) * GROUPS + occ, rep % 2
@@ -69,16 +69,20 @@
     contacts += [
         ((x, y, (z + d) % NZ, core), ready_z.at[NZ - d], (z + d) % NZ > z, core < 2) for d in Z_STEPS
     ]
+    contacts += [((x, y, z, 1 - core), ready_c, core == 0, core < 2)]
     barrier = pltpu.get_barrier_semaphore()
     sibling = at(x, y, z, 1 - core)
-    pl.semaphore_signal(barrier, inc=1, device_id=sibling, device_id_type=MESH)
     for where, _, later, other in contacts:
         @pl.when(later & other)
         def _(where=where):
             pl.semaphore_signal(barrier, inc=1, device_id=at(*where), device_id_type=MESH)
 
     lower = sum(((z + d) % NZ < z).astype(jnp.int32) for d in Z_STEPS)
-    pl.semaphore_wait(barrier, turn_x(x) + turn_y(y) + lower + 1)
+    before = turn_x(x) + turn_y(y) + lower + core
+
+    @pl.when(before > 0)
+    def _():
+        pl.semaphore_wait(barrier, before)
     for where, ready, later, other in contacts:
         @pl.when(jnp.logical_not(later) & other)
         def _(where=where, ready=ready):
@@ -200,7 +204,7 @@
     pl.when(jnp.logical_not(early))(prepare)
 
     def product(start):
-        block, rows = cbuf[start:start + NY], lad[start:start + NY]
+        block, rows = cbuf[pl.ds(start, NY)], lad[pl.ds(start, NY)]
 
         def dot(a, b):
             a, b = a.reshape(-1, LANES), b.reshape(-1, COLS)
@@ -211,18 +215,20 @@
         aside = [dot(block[:, j * step:(j + 1) * step], rows[:, MAIN:])[CAP:] for j in range(3)]
         return main + jnp.concatenate(aside, axis=0)
 
-    for x1 in range(NX):
-        @pl.when(x1 != x)
-        def _(x1=x1):
-            for y1 in range(NY):
-                c_wait(x1 * NY + y1)
-    racc[...] = product(0)
-    for x1 in range(1, NX):
-        racc[...] += product(x1 * NY)
+    racc[...] = product(x * NY)
+    for d in (1, 3, 2):
+        start = lax.rem(x + d, NX) * NY
+        for y1 in range(NY):
+            c_wait(start + y1)
+        racc[...] += product(start)
 
     mine = pl.ds(pl.multiple_of(core * HALF, HALF), HALF)
     theirs = pl.ds(pl.multiple_of((1 - core) * HALF, HALF), HALF)
     half_copy = copy(racc.at[theirs], rin, r_send, r_recv, sibling)
+
+    @pl.when(core == 0)
+    def _():
+        pl.semaphore_wait(ready_c, 1)
     half_copy.start()
     half_copy.wait_recv()
     total = racc[mine, :] + rin[...]
@@ -375,6 +381,7 @@
             pltpu.SemaphoreType.REGULAR((NX,)),
             pltpu.SemaphoreType.REGULAR((NY,)),
             pltpu.SemaphoreType.REGULAR((NZ,)),
+            pltpu.SemaphoreType.REGULAR,
         ],
         compiler_params=pltpu.CompilerParams(
             collective_id=0, has_side_effects=True, vmem_limit_bytes=48 * 1024 * 1024

time: 49.1 us -> 48.8 us (level)
  no operation moved by 1% of the time
where the time goes in v2:
time: 48.8 us; the launch traced here: 48.7 us
  Pallas kernels  47.1 us (97%)
  local copies, waits for them, and re-layouts  0.76 us (2%)
  between operations  0.67 us (1%)
    pallas_call x1, Pallas kernels, compact(): pl.pallas_call(kernel, out_shape=(jax.ShapeDtypeStruct((ROWS, COLS), BF),...  47.1 us

profile of v2, /device:TPU:1, one launch (start us, length us, event | category | flops | bytes accessed | tf_op | source)
XLA Modules:
  0.0 48.7 jit_solution(2797680050541614806)
XLA Ops:
  0.0 0.0 copy-start.1
  0.0 0.0 copy-start.2
  0.0 47.1 %shard_map.57 = (bf16[512,384]{1,0:T(8,128)(2,1)S(1)}, s32[1]{0:T(128)}) custom-call(bf16[96,512]{1,0:T(8,128)(2,1)} %bitcast.28, bf16[32,96,384]{2,1,0:T(8,128)(2,1)} %bitcast.31, bf16[512,3072]{1,0:T(8,128)(2,1)} %cyc_ref.1, s32[1,3072]{1,0:T(1,128)} %bitcast.30, s32[1,12288]{1,0:T(1,128)} %bitcast.29), custom_call_target="tpu_custom_call" | custom-call | flops 2000000000 | bytes 6500000 | tf_op jit(solution)/shard_map/pallas_call | solution.py:344
  47.7 0.0 copy-done.1
  47.7 0.0 copy-done.2
  47.7 0.2 conditional.1
  47.9 0.7 %copy.48 = bf16[512,384]{1,0:T(8,128)(2,1)} copy(bf16[512,384]{1,0:T(8,128)(2,1)S(1)} %get-tuple-element.361) | data formatting | bytes 786432
Async XLA Ops:
  0.0 47.7 %copy-start.1 = (bf16[512,96]{0,1:T(8,128)(2,1)S(1)}, bf16[512,96]{0,1:T(8,128)(2,1)}, u32[]{:S(2)}) copy-start(bf16[512,96]{0,1:T(8,128)(2,1)} %param.13) | copy-start | bytes 294916
  0.0 47.7 %copy-start.2 = (s32[3072]{0:T(1024)S(1)}, s32[3072]{0:T(1024)}, u32[]{:S(2)}) copy-start(s32[3072]{0:T(1024)} %param.16) | copy-start | bytes 36868
